TPU v7x, 256 devices: a whole 4x4x8 slice. The times are simulated.
256 devices in a mesh: grp: 8 (over x, core), shard: 32 (over z, y).
Axes of the slice: x: 4, y: 4, z: 8, core: 2. Of those that a mesh axis runs over, the one named last changes fastest.
Arguments:
- queries: bfloat16 [32768, 768], P(('grp', 'shard')), may hold values from -6 to 6
- positives: bfloat16 [32768, 768], P(('grp', 'shard')), may hold values from -6 to 6
- negative_ids: int32 [32768, 16], P(('grp', 'shard')), may hold values from 0 to 131071, as said below
- passage_table: bfloat16 [131072, 768], P('shard'), may hold values from -6 to 6
- inner_weight: bfloat16 [768, 2048], P('shard'), may hold values from -0.21875 to 0.21875
- outer_weight: bfloat16 [2048, 768], P('shard'), may hold values from -0.125 to 0.125
Outputs:
- loss_values: float32 [32768], P(('grp', 'shard'))
- inner_grad: float32 [768, 2048], P('shard')
- outer_grad: float32 [2048, 768], P('shard')
Inputs may be any that keep to these rules, and one draw needn't show every extreme that they name: `negative_ids`: the owner of a row id is id // 4096. The 2048 ids of one block of 128 consecutive queries name at most 128 rows of one owner; one owner gets exactly 128 from every block. Owners 2 j and 2 j + 1 form a pair, and each block names exactly 128 rows of each pair. Rows may repeat.
All inputs are finite; a program needn't handle non-finite values.
Results may differ from a plain program's by a relative error of at most 0.025.
Values may be sent and summed in bfloat16 or wider, within the bound.
No kernel may reach another device: no remote copies, remote signals or barrier semaphores. Data moves between devices by JAX's collectives and lax.ppermute only.
A program may use at most 128 MiB of HBM per device.

v0:
```python
import jax
import jax.numpy as jnp
from jax import lax
from jax.sharding import PartitionSpec as P


def gelu_value(pre_act):
    return pre_act * 0.5 * (1.0 + lax.erf(pre_act * 0.7071067811865476))


def gelu_slope(pre_act):
    return (
        0.5 * (1.0 + lax.erf(pre_act * 0.7071067811865476))
        + pre_act * jnp.exp(-0.5 * pre_act * pre_act) * 0.3989422804014327
    )


def softmax_terms(neg_scores, pos_scores):
    scores = jnp.concatenate([pos_scores[:, None], neg_scores], axis=1)
    log_total = jnp.log(jnp.sum(jnp.exp(scores), axis=1))
    losses = log_total - pos_scores
    score_grad = jnp.exp(scores - log_total[:, None]).at[:, 0].add(-1.0)
    return (losses, score_grad[:, 0], score_grad[:, 1:])


def contract_first(left, right):
    return lax.dot_general(
        left, right, (((0,), (0,)), ((), ())), preferred_element_type=jnp.float32
    )


def contract_last(left, right):
    return lax.dot_general(
        left, right, (((1,), (1,)), ((), ())), preferred_element_type=jnp.float32
    )


def bucket_ranks(labels, count):
    member = (labels[:, None] == jnp.arange(count, dtype=jnp.int32)[None, :]).astype(jnp.int32)
    return jnp.sum((jnp.cumsum(member, axis=0) - 1) * member, axis=1)


def shards(queries, positives, negative_ids, passage_table, inner_weight, outer_weight):
    q_dev, width = queries.shape
    neg_count = negative_ids.shape[1]
    rows_dev = passage_table.shape[0]
    n_shard = lax.axis_size("shard")
    capacity = 2 * q_dev * neg_count // n_shard
    scale = float(width) ** (-0.5)
    columns = queries
    pre_act = jnp.dot(
        columns,
        lax.all_gather(inner_weight, "shard", axis=0, tiled=True),
        preferred_element_type=jnp.float32,
    )
    hidden = gelu_value(pre_act).astype(jnp.bfloat16)
    columns = hidden
    projected = jnp.dot(
        columns,
        lax.all_gather(outer_weight, "shard", axis=0, tiled=True),
        preferred_element_type=jnp.float32,
    )
    embedded = (queries.astype(jnp.float32) + projected).astype(jnp.bfloat16)
    pos_scores = (
        jnp.einsum("qd,qd->q", embedded, positives, preferred_element_type=jnp.float32) * scale
    )
    flat_ids = negative_ids.reshape(-1)
    owners = flat_ids // rows_dev
    local_rows = flat_ids - owners * rows_dev
    slot_of = owners * capacity + bucket_ranks(owners, n_shard)
    requests = (
        jnp.zeros((n_shard * capacity,), jnp.int32)
        .at[slot_of]
        .set(local_rows)
        .reshape(n_shard, capacity)
    )
    found_rows = jnp.take(
        passage_table,
        lax.all_to_all(requests, "shard", split_axis=0, concat_axis=0, tiled=True),
        axis=0,
    )
    fetched = lax.all_to_all(found_rows, "shard", split_axis=0, concat_axis=0, tiled=True).reshape(
        -1, width
    )
    negatives = jnp.take(fetched, slot_of, axis=0).reshape(q_dev, neg_count, width)
    neg_scores = (
        jnp.einsum("qkd,qd->qk", negatives, embedded, preferred_element_type=jnp.float32) * scale
    )
    losses, pos_grad, neg_grad = softmax_terms(neg_scores, pos_scores)
    neg_term = (
        jnp.einsum(
            "qk,qkd->qd", neg_grad, negatives.astype(jnp.float32), precision=lax.Precision.HIGHEST
        )
        * scale
    )
    query_grad = (neg_term + scale * pos_grad[:, None] * positives.astype(jnp.float32)).astype(
        jnp.bfloat16
    )
    hidden_grad = contract_last(
        query_grad, lax.all_gather(outer_weight, "shard", axis=0, tiled=True)
    )
    pre_grad = (hidden_grad * gelu_slope(pre_act)).astype(jnp.bfloat16)
    columns = queries
    inner_part = lax.psum_scatter(
        contract_first(columns, pre_grad).astype(jnp.bfloat16),
        "shard",
        scatter_dimension=0,
        tiled=True,
    )
    columns = hidden
    outer_part = lax.psum_scatter(
        contract_first(columns, query_grad).astype(jnp.bfloat16),
        "shard",
        scatter_dimension=0,
        tiled=True,
    )
    inner_grad, outer_grad = (
        lax.psum(inner_part, "grp").astype(jnp.float32),
        lax.psum(outer_part, "grp").astype(jnp.float32),
    )
    return (losses, inner_grad, outer_grad)


def solution(mesh):
    placed = (
        P(("grp", "shard"), None),
        P(("grp", "shard"), None),
        P(("grp", "shard"), None),
        P("shard", None),
        P("shard", None),
        P("shard", None),
    )
    return jax.shard_map(
        shards,
        mesh=mesh,
        in_specs=placed,
        out_specs=(P(("grp", "shard")), P("shard", None), P("shard", None)),
        check_vma=False,
    )
```

profile of v0, /device:TPU:1, one launch (start us, length us, event | category | flops | bytes accessed | tf_op | source)
XLA Modules:
  0.0 809.3 jit_solution(1007956227018702688)
XLA Ops:
  7.2 0.8 copy.21
  8.0 0.1 reshape.214
  8.0 0.1 reshape.213
  8.1 0.1 reshape.216
  8.3 9.1 %reduce-window.6 = s32[32,16,128]{2,1,0:T(8,128)S(1)} reduce-window(s32[32,16,128]{2,1,0:T(8,128)S(1)} %fusion.22, s32[]{:T(128)} %constant.89.clone.1), window={size=1x1x128 pad=0_0x0_0x127_0}, to_apply=%region_0.1 | reduce-window | flops 8323072 | bytes 524292 | tf_op jit(solution)/shard_map/reduce-window
  17.3 0.1 slice.38
  17.5 0.2 copy.40
  17.7 0.2 reduce-window.9
  17.9 0.1 add_add_fusion
  18.1 0.1 fusion.21
  18.2 0.1 compare_select_fusion.1
  18.3 8.6 %scatter_custom_fusion = s32[4096]{0:T(1024)} fusion(s32[2048]{0:T(1024)S(1)} %bitcast.63, s32[2048]{0:T(1024)S(1)} %get-tuple-element.26, s32[]{:T(128)} %constant.89.clone.1), kind=kCustom, calls=%fused_computation.78 | custom fusion | bytes 16388 | tf_op jit(solution)/shard_map/scatter | solution.py:74
  26.9 12.0 %all-to-all-start = ((s32[32,1,128]{2,1,0:T(1,128)}), s32[32,1,128]{2,1,0:T(1,128)S(1)}, u32[]{:S(2)}, u32[]{:S(2)}) async-start(s32[32,1,128]{2,1,0:T(1,128)} %bitcast.6), calls=%async_computation | async-start | bytes 32768 | tf_op jit(solution)/shard_map/all_to_all | solution.py:79
  38.9 0.0 all-gather.3.cloned.1.call-start
  39.0 0.7 all-gather.3.cloned.1.call-update
  39.7 7.8 all-to-all-done
  47.4 22.7 %gather_fusion = bf16[4096,768]{1,0:T(8,128)(2,1)} fusion(bf16[4096,768]{1,0:T(8,128)(2,1)} %param.11, s32[4096]{0:T(1024)S(1)} %fusion.28), kind=kCustom, calls=%fused_computation | custom fusion | bytes 12599296 | tf_op jit(solution)/shard_map/jit(_take)/gather | solution.py:77
  70.1 6.6 broadcast_select_fusion
  76.7 5.0 all-to-all-start.1
  81.7 0.0 all-gather.5.cloned.1.call-start
  81.8 0.7 all-gather.5.cloned.1.call-update
  82.5 0.0 reduce-scatter.7.cloned.1.call-start
  82.5 0.1 reduce_sum.23
  82.6 0.6 compare_reduce_fusion
  83.3 0.1 compare_and_fusion
  83.3 80.7 %all-gather.3.cloned.1.call-done = bf16[768,2048]{1,0:T(8,128)(2,1)} async-done(((bf16[24,2048]{1,0:T(8,128)(2,1)}), bf16[768,2048]{1,0:T(8,128)(2,1)}) %all-gather.3.cloned.1.call-update) | async-done | bytes 3145744 | tf_op jit(solution)/shard_map/all_gather | solution.py:53
  164.0 2.5 fusion.46
  166.5 91.3 %all-gather.5.cloned.1.call-done = bf16[2048,768]{1,0:T(8,128)(2,1)} async-done(((bf16[64,768]{1,0:T(8,128)(2,1)}), bf16[2048,768]{1,0:T(8,128)(2,1)}) %all-gather.5.cloned.1.call-update) | async-done | bytes 3145744 | tf_op jit(solution)/shard_map/all_gather | solution.py:60
  257.8 2.6 fusion.16
  260.4 13.7 %gather_fusion.1 = bf16[2048,768]{1,0:T(8,128)(2,1)} fusion(bf16[4096,768]{1,0:T(8,128)(2,1)} %bitcast.11, s32[2048]{0:T(1024)S(1)} %broadcast_clamp_fusion), kind=kCustom, calls=%fused_computation.1 | custom fusion | bytes 6299648 | tf_op jit(solution)/shard_map/jit(_take)/gather | solution.py:85
  274.1 3.1 fusion.2
  277.2 0.1 copy.36
  277.3 0.5 fusion.42
  277.9 0.1 copy.37
  278.0 3.4 fusion.1
  281.4 0.7 fusion.36
  282.1 5.6 fusion
  287.7 4.8 copy.41
  292.5 0.0 reduce-scatter.7.cloned.1.call-update
  292.5 0.0 reduce-scatter.5.cloned.1.call-start
  292.6 2.8 convolution_convert_fusion
  295.4 0.0 all-reduce.3.cloned.1.call-start
  295.4 211.9 %reduce-scatter.7.cloned.1.call-done = bf16[24,2048]{1,0:T(8,128)(2,1)} async-done(((bf16[768,2048]{1,0:T(8,128)(2,1)}), bf16[24,2048]{1,0:T(8,128)(2,1)}) %reduce-scatter.7.cloned.1.call-update) | async-done | bytes 98320
  507.4 1.9 copy.42
  509.3 220.1 %reduce-scatter.5.cloned.1.call-done = bf16[64,768]{1,0:T(8,128)(2,1)} async-done(((bf16[2048,768]{1,0:T(8,128)(2,1)}), bf16[64,768]{1,0:T(8,128)(2,1)}) %reduce-scatter.5.cloned.1.call-update) | async-done | bytes 98320 | tf_op jit(solution)/shard_map/reduce_scatter | solution.py:111
  729.4 69.8 %all-reduce.3.cloned.1.call-done = (bf16[24,2048]{0,1:T(8,128)(2,1)}, bf16[64,768]{1,0:T(8,128)(2,1)}) async-done(((bf16[24,2048]{0,1:T(8,128)(2,1)}, bf16[64,768]{1,0:T(8,128)(2,1)}), (bf16[24,2048]{0,1:T(8,128)(2,1)}, bf16[64,768]{1,0:T(8,128)(2,1)})) %all-reduce.3.cloned.1.call-update) | async-done | bytes 196624 | tf_op jit(solution)/shard_map/psum | solution.py:118
  799.3 1.6 convert_element_type.50
  800.8 1.9 copy.30
  (18 shorter events, 0.2 us)
Async XLA Ops:
  26.9 20.5 %all-to-all-start = ((s32[32,1,128]{2,1,0:T(1,128)}), s32[32,1,128]{2,1,0:T(1,128)S(1)}, u32[]{:S(2)}, u32[]{:S(2)}) async-start(s32[32,1,128]{2,1,0:T(1,128)} %bitcast.6), calls=%async_computation | async-start | bytes 32768 | tf_op jit(solution)/shard_map/all_to_all | solution.py:79
  38.9 125.1 %all-gather.3.cloned.1.call-start = ((), (), s32[]{:S(2)}) async-start(), calls=%async_computation.4 | async-start | bytes 3244032 | tf_op jit(solution)/shard_map/all_gather | solution.py:53
  76.7 87.3 %copy-start = (bf16[128,768]{1,0:T(8,128)(2,1)S(1)}, bf16[128,768]{1,0:T(8,128)(2,1)}, u32[]{:S(2)}) copy-start(bf16[128,768]{1,0:T(8,128)(2,1)} %param.8) | copy-start | bytes 589828
  76.7 183.7 %all-to-all-start.1 = ((bf16[32,128,768]{2,1,0:T(8,128)(2,1)}), bf16[32,128,768]{2,1,0:T(8,128)(2,1)}, u32[]{:S(2)}, u32[]{:S(2)}) async-start(bf16[32,128,768]{2,1,0:T(8,128)(2,1)} %broadcast_select_fusion), calls=%async_computation.1 | async-start | bytes 12582912 | tf_op jit(solution)/shard_map/all_to_all | solution.py:82
  81.7 176.0 %copy-start.1 = (bf16[128,768]{1,0:T(8,128)(2,1)S(1)}, bf16[128,768]{1,0:T(8,128)(2,1)}, u32[]{:S(2)}) copy-start(bf16[128,768]{1,0:T(8,128)(2,1)} %param.9) | copy-start | bytes 589828
  81.7 176.0 %all-gather.5.cloned.1.call-start = ((), (), s32[]{:S(2)}) async-start(), calls=%async_computation.5 | async-start | bytes 3244032 | tf_op jit(solution)/shard_map/all_gather | solution.py:60
  82.5 424.9 %reduce-scatter.7.cloned.1.call-start = ((), (), s32[]{:S(2)}) async-start(), calls=%async_computation.7 | async-start | bytes 3244032
  292.5 436.9 %reduce-scatter.5.cloned.1.call-start = ((), (), s32[]{:S(2)}) async-start(), calls=%async_computation.6 | async-start | bytes 3244032 | tf_op jit(solution)/shard_map/reduce_scatter | solution.py:111
  295.4 503.9 %all-reduce.3.cloned.1.call-start = ((), (), s32[]{:S(2)}) async-start(), calls=%async_computation.8 | async-start | bytes 1245184 | tf_op jit(solution)/shard_map/psum | solution.py:118
Sparse Core Ops, SparseCore 0:
  42.3 121.6 all-gather.2
  166.6 91.1 all-gather.4
  292.6 214.6 reduce-scatter.6
  511.6 217.7 reduce-scatter.4
  731.7 67.5 all-reduce.2
where the time goes:
time: 811 us; the launch traced here: 809 us
  waiting for transfers between devices  683 us (84%)
  local copies, waits for them, and re-layouts  55.2 us (7%)
  matrix products  20.1 us (2%)
  other arithmetic  19.8 us (2%)
  starting transfers between devices  17.3 us (2%)
  between operations  13.9 us (2%)
    reduce_scatter x1, waiting for transfers between devices, shards(): lax.psum_scatter(contract_first(columns, query_grad).astype(jnp.bfloat16)...  220 us
    unnamed x6, waiting for transfers between devices  213 us
    all_gather x1, waiting for transfers between devices, shards(): lax.all_gather(outer_weight, 'shard', axis=0, tiled=True)  91.3 us
    all_gather x1, waiting for transfers between devices, shards(): lax.all_gather(inner_weight, 'shard', axis=0, tiled=True)  80.7 us
    psum x1, waiting for transfers between devices, shards(): lax.psum(inner_part, 'grp').astype(jnp.float32)  69.8 us
    gather x1, local copies, waits for them, and re-layouts, shards(): jnp.take(passage_table, lax.all_to_all(requests, 'shard', split_axis=0, c...  22.7 us
  transfers between devices with their start and end apart: 7, of which 6 were waited for; matrix products, arithmetic and copies ran while one was open for 5% of the time, Pallas kernels for 0%

commit v1 on v0

v1 whole, which is shorter than its diff:
```python
import functools

import jax
import jax.numpy as jnp
from jax import lax
from jax.experimental import pallas as pl
from jax.experimental.pallas import tpu as pltpu
from jax.sharding import Mesh, PartitionSpec as P

X, CORE, Z, Y = 4, 2, 8, 4
GRP, SHARD = X * CORE, Z * Y
PAIRS = SHARD // 2
CHUNKS = 4
VMEM = 50 * 1024 * 1024


def gelu_value(pre_act):
    return pre_act * 0.5 * (1.0 + lax.erf(pre_act * 0.7071067811865476))


def gelu_slope(pre_act):
    return (
        0.5 * (1.0 + lax.erf(pre_act * 0.7071067811865476))
        + pre_act * jnp.exp(-0.5 * pre_act * pre_act) * 0.3989422804014327
    )


def contract_first(left, right):
    return lax.dot_general(
        left, right, (((0,), (0,)), ((), ())), preferred_element_type=jnp.float32
    )


def contract_last(left, right):
    return lax.dot_general(
        left, right, (((1,), (1,)), ((), ())), preferred_element_type=jnp.float32
    )


def exchange(value, axes):
    return lax.all_to_all(value, axes, split_axis=0, concat_axis=0, tiled=True)


def spread(value, axes, count):
    return exchange(jnp.broadcast_to(value[None], (count, *value.shape)), axes)


def request_kernel(shift, ids_ref, rows_ref, even_ref, query_ref):
    ids = ids_ref[...]
    q_dev, neg = ids.shape
    lane = lax.broadcasted_iota(jnp.int32, (q_dev, q_dev), 1)
    query = lax.broadcasted_iota(jnp.int32, (q_dev, q_dev), 0)
    before = (lane < query).astype(jnp.float32).astype(jnp.bfloat16)
    kind, pair_lane = lane // PAIRS, lane % PAIRS
    seen = jnp.zeros((1, q_dev), jnp.float32)
    placed = jnp.zeros((q_dev, q_dev), jnp.float32)
    for k in range(neg):
        id_k = ids[:, k : k + 1]
        owner = id_k >> shift
        odd = owner & 1
        member = owner == lane
        ones = member.astype(jnp.float32)
        counts = seen + jnp.dot(before, ones.astype(jnp.bfloat16), preferred_element_type=jnp.float32)
        rank = jnp.sum(jnp.where(member, counts, 0.0), axis=1, keepdims=True).astype(jnp.int32)
        seen = seen + jnp.sum(ones, axis=0, keepdims=True)
        slot = jnp.where(odd == 1, q_dev - 1 - rank, rank)
        at_slot = (slot == lane).astype(jnp.float32).astype(jnp.bfloat16)
        code = (odd << shift) + (id_k - (owner << shift))
        item = jnp.where(
            kind == 0, code >> 6, jnp.where(kind == 1, code & 63, jnp.where(kind == 2, query, 0))
        )
        item = jnp.where((owner >> 1) == pair_lane, item, 0)
        placed = placed + contract_first(item.astype(jnp.float32).astype(jnp.bfloat16), at_slot)
    code = (placed[:PAIRS] * 64.0 + placed[PAIRS : 2 * PAIRS]).astype(jnp.int32)
    rows_ref[...] = code & ((1 << shift) - 1)
    even_ref[...] = 1 - (code >> shift)
    query_ref[...] = placed[2 * PAIRS : 3 * PAIRS].astype(jnp.int32)


def score_kernel(scale, embedded_ref, positives_ref, hidden_ref, query_ref, *refs):
    row_refs, (loss_ref, grad_ref, outer_ref) = refs[:CHUNKS], refs[CHUNKS:]
    embedded = embedded_ref[...]
    positives = positives_ref[...].astype(jnp.float32)
    q_dev, width = embedded.shape
    pos_scores = (
        jnp.sum(embedded.astype(jnp.float32) * positives, axis=1, keepdims=True) * scale
    )
    total = jnp.exp(pos_scores)
    per = row_refs[0].shape[0]
    query = lax.broadcasted_iota(jnp.int32, (q_dev, per), 0)
    scores, members = [], []
    for c in range(CHUNKS):
        score = contract_last(embedded, row_refs[c][...]) * scale
        member = query_ref[:, c * per : (c + 1) * per] == query
        total = total + jnp.sum(jnp.where(member, jnp.exp(score), 0.0), axis=1, keepdims=True)
        scores.append(score)
        members.append(member)
    log_total = jnp.log(total)
    loss_ref[...] = log_total - pos_scores
    grad = (jnp.exp(pos_scores - log_total) - 1.0) * positives
    for c in range(CHUNKS):
        weight = jnp.where(members[c], jnp.exp(scores[c] - log_total), 0.0)
        high = weight.astype(jnp.bfloat16)
        low = (weight - high.astype(jnp.float32)).astype(jnp.bfloat16)
        rows = row_refs[c][...]
        grad = grad + jnp.dot(high, rows, preferred_element_type=jnp.float32)
        grad = grad + jnp.dot(low, rows, preferred_element_type=jnp.float32)
    query_grad = (grad * scale).astype(jnp.bfloat16)
    grad_ref[...] = query_grad
    hid = hidden_ref.shape[1]
    deep, part, half = hid // SHARD // X, hid // Z, width // CORE
    for z in range(Z):
        outer = contract_first(hidden_ref[:, z * part : (z + 1) * part], query_grad).astype(
            jnp.bfloat16
        )
        for y in range(Y):
            for x in range(X):
                rows = outer[(y * X + x) * deep : (y * X + x + 1) * deep]
                at = (x * Z + z) * deep
                for core in range(CORE):
                    outer_ref[core, y, at : at + deep, :] = rows[:, core * half : (core + 1) * half]


def inner_kernel(queries_ref, grad_ref, slope_ref, weight_ref, inner_ref):
    queries, query_grad = queries_ref[...], grad_ref[...]
    part = weight_ref.shape[0] // GRP
    for x in range(X):
        for core in range(CORE):
            at = (x * CORE + core) * part
            hidden_grad = contract_last(query_grad, weight_ref[at : at + part, :])
            pre_grad = (hidden_grad * slope_ref[:, at : at + part]).astype(jnp.bfloat16)
            inner_ref[core, x] = contract_first(queries, pre_grad).astype(jnp.bfloat16)


def total_of(parts, dtype=jnp.bfloat16):
    return jnp.sum(parts.astype(jnp.float32), axis=0).astype(dtype)


def shards(queries, positives, negative_ids, passage_table, inner_weight, outer_weight):
    q_dev, width = queries.shape
    rows_dev = passage_table.shape[0]
    hid = inner_weight.shape[1]
    inner_rows, outer_rows = inner_weight.shape[0], outer_weight.shape[0]
    scale = float(width) ** (-0.5)
    call = functools.partial(
        pl.pallas_call, compiler_params=pltpu.CompilerParams(vmem_limit_bytes=VMEM)
    )
    group = lax.axis_index("x") * CORE + lax.axis_index("core")

    slots = jax.ShapeDtypeStruct((PAIRS, q_dev), jnp.int32)
    wanted, even, slot_query = call(
        functools.partial(request_kernel, rows_dev.bit_length() - 1), out_shape=[slots] * 3
    )(negative_ids)
    requests = exchange(
        jnp.broadcast_to(wanted[:, None], (PAIRS, 2, q_dev)).reshape(SHARD, q_dev), ("z", "y")
    )
    requests = requests.reshape(Z, Y, q_dev).transpose(1, 0, 2)
    even = exchange(even, "z").reshape(Z, 2, q_dev).transpose(1, 0, 2)

    per = q_dev // CHUNKS
    chunks = []
    for c in range(CHUNKS):
        ids = requests[:, :, c * per : (c + 1) * per].reshape(-1)
        found = passage_table.at[ids].get(mode="promise_in_bounds")
        near = exchange(found, "y").reshape(2, 2, Z, per, width)
        merged = jnp.where(
            even[:, :, c * per : (c + 1) * per, None] == 1, near[:, 0], near[:, 1]
        )
        merged = merged.transpose(1, 0, 2, 3).reshape(-1, width)
        chunks.append(exchange(merged, "z"))
    slot_query = jnp.concatenate(
        [slot_query[:, c * per : (c + 1) * per].reshape(1, -1) for c in range(CHUNKS)], axis=1
    )

    wide = hid // GRP
    inner_piece = lax.dynamic_slice(inner_weight, (0, group * wide), (inner_rows, wide))
    blocks = width // wide
    deep = outer_rows * blocks // GRP
    outer_piece = lax.dynamic_slice(
        outer_weight.reshape(outer_rows, blocks, wide).transpose(1, 0, 2).reshape(-1, wide),
        (group * deep, 0),
        (deep, wide),
    )
    piece = jnp.concatenate([inner_piece, outer_piece], axis=0)
    gathered = spread(piece, ("z", "y"), SHARD)
    gathered = spread(gathered, "x", X)
    gathered = spread(gathered, "core", CORE).reshape(CORE, X, SHARD, inner_rows + deep, wide)
    inner_full = gathered[:, :, :, :inner_rows].transpose(2, 3, 1, 0, 4).reshape(-1, hid)
    outer_full = (
        gathered[:, :, :, inner_rows:]
        .transpose(2, 1, 0, 3, 4)
        .reshape(SHARD, blocks, outer_rows, wide)
        .transpose(0, 2, 1, 3)
        .reshape(hid, width)
    )

    pre_act = jnp.dot(queries, inner_full, preferred_element_type=jnp.float32)
    hidden = gelu_value(pre_act).astype(jnp.bfloat16)
    slope = gelu_slope(pre_act)
    projected = jnp.dot(hidden, outer_full, preferred_element_type=jnp.float32)
    embedded = (queries.astype(jnp.float32) + projected).astype(jnp.bfloat16)

    losses, query_grad, outer = call(
        functools.partial(score_kernel, scale),
        out_shape=[
            jax.ShapeDtypeStruct((q_dev, 1), jnp.float32),
            jax.ShapeDtypeStruct((q_dev, width), jnp.bfloat16),
            jax.ShapeDtypeStruct((CORE, Y, hid // Y, width // CORE), jnp.bfloat16),
        ],
    )(embedded, positives, hidden, slot_query, *chunks)
    inner = call(
        inner_kernel,
        out_shape=jax.ShapeDtypeStruct((CORE, X, width, wide), jnp.bfloat16),
    )(queries, query_grad, slope, outer_full)

    outer = total_of(exchange(outer, "core"))
    inner = total_of(exchange(inner, "core"))
    outer = total_of(exchange(outer, "y")).reshape(X, -1, width // CORE)
    inner = total_of(exchange(inner, "x"))
    outer = total_of(exchange(outer, "x")).reshape(Z, -1, width // CORE)
    inner = exchange(inner.reshape(SHARD, inner_rows, wide), ("z", "y"))
    outer = total_of(exchange(outer, "z"), jnp.float32)
    inner = total_of(inner, jnp.float32)
    outer = spread(outer, ("x", "core"), GRP)
    inner = spread(inner, ("x", "core"), GRP)
    outer = (
        outer.reshape(X, CORE, -1, width // CORE).transpose(0, 2, 1, 3).reshape(outer_rows, width)
    )
    inner = inner.transpose(1, 0, 2).reshape(inner_rows, hid)
    return (losses.reshape(-1), inner, outer)


def solution(mesh):
    fine = Mesh(mesh.devices.reshape(X, CORE, Z, Y), ("x", "core", "z", "y"))
    blocks, rows = ("x", "core", "z", "y"), ("z", "y")
    return jax.shard_map(
        shards,
        mesh=fine,
        in_specs=(
            P(blocks, None),
            P(blocks, None),
            P(blocks, None),
            P(rows, None),
            P(rows, None),
            P(rows, None),
        ),
        out_specs=(P(blocks), P(rows, None), P(rows, None)),
        check_vma=False,
    )
```

time: 811 us -> 444 us (0.55)
  waiting for transfers between devices: 683 us -> 166 us
  blocking collectives: 0 us -> 71.9 us
  starting transfers between devices: 17.3 us -> 82.4 us
  local copies, waits for them, and re-layouts: 55.2 us -> 81.2 us
  Pallas kernels: 0 us -> 19.3 us
  matrix products: 20.1 us -> 2.54 us
  between operations: 13.9 us -> 1.01 us
    reduce_scatter x1 -> x0, waiting for transfers between devices: 220 us -> none  [shards(): lax.psum_scatter(contract_first(columns, query_grad).astype(jnp.bfloat16)...]
    unnamed x6 -> x0, waiting for transfers between devices: 213 us -> none
    all_gather x2 -> x0, waiting for transfers between devices: 172 us -> none  [the longest x1 91.3 us: shards(): lax.all_gather(outer_weight, 'shard', axis=0, tiled=True)]
    all_to_all x2 -> x18, waiting for transfers between devices: 7.77 us -> 166 us  [exchange(): return lax.all_to_all(value, axes, split_axis=0, concat_axis=0, tiled=True)]
    all_to_all x0 -> x4, blocking collectives: none -> 71.9 us  [exchange(): return lax.all_to_all(value, axes, split_axis=0, concat_axis=0, tiled=True)]
    psum x1 -> x0, waiting for transfers between devices: 69.8 us -> none  [shards(): lax.psum(inner_part, 'grp').astype(jnp.float32)]
    all_to_all x2 -> x18, starting transfers between devices: 17.1 us -> 82.4 us  [exchange(): return lax.all_to_all(value, axes, split_axis=0, concat_axis=0, tiled=True)]
    pallas_call x0 -> x3, Pallas kernels: none -> 19.3 us  [the longest x1 6.82 us: shards(): call(functools.partial(score_kernel, scale), out_shape=[jax.ShapeDtypeStr...]
  transfers between devices with their start and end apart: 7 -> 18, of which waited for: 6 -> 16; matrix products, arithmetic and copies ran while one was open for 5% -> 19% of each run, Pallas kernels for 0% -> 1%
where the time goes in v1:
time: 444 us; the launch traced here: 442 us
  waiting for transfers between devices  166 us (37%)
  starting transfers between devices  82.4 us (19%)
  local copies, waits for them, and re-layouts  81.2 us (18%)
  blocking collectives  71.9 us (16%)
  Pallas kernels  19.3 us (4%)
  other arithmetic  17.6 us (4%)
    all_to_all x18, waiting for transfers between devices, exchange(): return lax.all_to_all(value, axes, split_axis=0, concat_axis=0, tiled=True)  166 us
    all_to_all x18, starting transfers between devices, exchange(): return lax.all_to_all(value, axes, split_axis=0, concat_axis=0, tiled=True)  82.4 us
    all_to_all x4, blocking collectives, exchange(): return lax.all_to_all(value, axes, split_axis=0, concat_axis=0, tiled=True)  71.9 us
    gather x4, local copies, waits for them, and re-layouts, shards(): found = passage_table.at[ids].get(mode='promise_in_bounds')  36.7 us
    reduce_sum x7, other arithmetic, total_of(): return jnp.sum(parts.astype(jnp.float32), axis=0).astype(dtype)  12.6 us
  transfers between devices with their start and end apart: 18, of which 16 were waited for; matrix products, arithmetic and copies ran while one was open for 19% of the time, Pallas kernels for 1%

profile of v1, /device:TPU:1, one launch (start us, length us, event | category | flops | bytes accessed | tf_op | source)
XLA Modules:
  0.0 441.7 jit_solution(14368320433103292130)
XLA Ops:
  1.4 6.5 %shard_map.85 = (s32[16,128]{1,0:T(8,128)S(1)}, s32[16,128]{1,0:T(8,128)}, s32[16,128]{1,0:T(8,128)S(1)}) custom-call(s32[128,16]{1,0:T(8,128)S(1)} %copy.97.ids_ref), custom_call_target="tpu_custom_call" | custom-call | tf_op jit(solution)/shard_map/pallas_call | solution.py:151
  7.9 20.4 %all_to_all.158 = s32[32,1,128]{2,1,0:T(1,128)S(1)} all-to-all(s32[32,1,128]{2,1,0:T(1,128)S(1)} %bitcast.119), channel_id=1, replica_groups=mesh['x'=4,'core'=2,'z'=8,'y'=4] {'z','y'}, dimensions={0} | all-to-all | bytes 32768 | tf_op jit(solution)/shard_map/all_to_all | solution.py:41
  31.9 9.2 %gather_fusion = bf16[1024,768]{1,0:T(8,128)(2,1)} fusion(bf16[4096,768]{1,0:T(8,128)(2,1)} %param.9, s32[1024]{0:T(1024)S(1)} %broadcast_clamp_fusion.3), kind=kCustom, calls=%fused_computation | custom fusion | bytes 3149824 | tf_op jit(solution)/shard_map/gather | solution.py:164
  41.1 3.6 all-to-all-start.5
  44.8 9.2 %gather_fusion.1 = bf16[1024,768]{1,0:T(8,128)(2,1)} fusion(bf16[4096,768]{1,0:T(8,128)(2,1)} %param.9, s32[1024]{0:T(1024)S(1)} %broadcast_clamp_fusion.2), kind=kCustom, calls=%fused_computation.1 | custom fusion | bytes 3149824 | tf_op jit(solution)/shard_map/gather | solution.py:164
  53.9 9.3 %all-to-all-done.5 = bf16[4,256,768]{2,1,0:T(8,128)(2,1)S(1)} async-done(((bf16[4,256,768]{2,1,0:T(8,128)(2,1)}), bf16[4,256,768]{2,1,0:T(8,128)(2,1)S(1)}, u32[]{:S(2)}, u32[]{:S(2)}) %all-to-all-start.5) | async-done | bytes 1572896 | tf_op jit(solution)/shard_map/all_to_all | solution.py:41
  63.2 3.6 all-to-all-start.7
  66.9 9.2 %gather_fusion.2 = bf16[1024,768]{1,0:T(8,128)(2,1)} fusion(bf16[4096,768]{1,0:T(8,128)(2,1)} %param.9, s32[1024]{0:T(1024)S(1)} %broadcast_clamp_fusion.1), kind=kCustom, calls=%fused_computation.2 | custom fusion | bytes 3149824 | tf_op jit(solution)/shard_map/gather | solution.py:164
  76.1 8.4 %all-to-all-done.7 = bf16[4,256,768]{2,1,0:T(8,128)(2,1)S(1)} async-done(((bf16[4,256,768]{2,1,0:T(8,128)(2,1)}), bf16[4,256,768]{2,1,0:T(8,128)(2,1)S(1)}, u32[]{:S(2)}, u32[]{:S(2)}) %all-to-all-start.7) | async-done | bytes 1572896 | tf_op jit(solution)/shard_map/all_to_all | solution.py:41
  85.7 3.6 all-to-all-start.9
  89.4 9.2 %gather_fusion.3 = bf16[1024,768]{1,0:T(8,128)(2,1)} fusion(bf16[4096,768]{1,0:T(8,128)(2,1)} %param.9, s32[1024]{0:T(1024)S(1)} %broadcast_clamp_fusion), kind=kCustom, calls=%fused_computation.3 | custom fusion | bytes 3149824 | tf_op jit(solution)/shard_map/gather | solution.py:164
  98.5 7.2 %all-to-all-done.9 = bf16[4,256,768]{2,1,0:T(8,128)(2,1)S(1)} async-done(((bf16[4,256,768]{2,1,0:T(8,128)(2,1)}), bf16[4,256,768]{2,1,0:T(8,128)(2,1)S(1)}, u32[]{:S(2)}, u32[]{:S(2)}) %all-to-all-start.9) | async-done | bytes 1572896 | tf_op jit(solution)/shard_map/all_to_all | solution.py:41
  105.7 4.4 all-to-all-start.11
  110.9 14.5 %all-to-all-done.11 = bf16[4,256,768]{2,1,0:T(8,128)(2,1)} async-done(((bf16[4,256,768]{2,1,0:T(8,128)(2,1)}), bf16[4,256,768]{2,1,0:T(8,128)(2,1)}, u32[]{:S(2)}, u32[]{:S(2)}) %all-to-all-start.11) | async-done | bytes 1572896 | tf_op jit(solution)/shard_map/all_to_all | solution.py:41
  126.4 6.5 %all-to-all-start = ((bf16[32,48,256]{2,1,0:T(8,128)(2,1)}), bf16[32,48,256]{2,1,0:T(8,128)(2,1)}, u32[]{:S(2)}, u32[]{:S(2)}) async-start(bf16[32,48,256]{2,1,0:T(8,128)(2,1)} %broadcast_in_dim.35), calls=%async_computation | async-start | bytes 1572864 | tf_op jit(solution)/shard_map/all_to_all | solution.py:41
  134.2 13.8 %all-to-all-done = bf16[32,48,256]{2,1,0:T(8,128)(2,1)} async-done(((bf16[32,48,256]{2,1,0:T(8,128)(2,1)}), bf16[32,48,256]{2,1,0:T(8,128)(2,1)}, u32[]{:S(2)}, u32[]{:S(2)}) %all-to-all-start) | async-done | bytes 786464 | tf_op jit(solution)/shard_map/all_to_all | solution.py:41
  148.0 3.9 all-to-all-start.6
  154.5 12.6 %all-to-all-done.6 = bf16[8,64,768]{2,1,0:T(8,128)(2,1)S(1)} async-done(((bf16[8,64,768]{2,1,0:T(8,128)(2,1)}), bf16[8,64,768]{2,1,0:T(8,128)(2,1)S(1)}, u32[]{:S(2)}, u32[]{:S(2)}) %all-to-all-start.6) | async-done | bytes 786464 | tf_op jit(solution)/shard_map/all_to_all | solution.py:41
  167.1 18.4 %all_to_all.159 = bf16[8,64,768]{2,1,0:T(8,128)(2,1)S(1)} all-to-all(bf16[8,64,768]{2,1,0:T(8,128)(2,1)} %bitcast.109), channel_id=1, replica_groups=mesh['x'=4,'core'=2,'z'=8,'y'=4] {'z'}, dimensions={0} | all-to-all | bytes 1572864 | tf_op jit(solution)/shard_map/all_to_all | solution.py:41
  188.6 4.7 %all-to-all-start.1 = ((bf16[4,32,48,256]{3,2,1,0:T(8,128)(2,1)}), bf16[4,32,48,256]{3,2,1,0:T(8,128)(2,1)}, u32[]{:S(2)}, u32[]{:S(2)}) async-start(bf16[4,32,48,256]{3,2,1,0:T(8,128)(2,1)} %broadcast_in_dim.36), calls=%async_computation.1 | async-start | bytes 6291456 | tf_op jit(solution)/shard_map/all_to_all | solution.py:41
  194.4 25.4 %all-to-all-done.1 = bf16[4,32,48,256]{3,2,1,0:T(8,128)(2,1)} async-done(((bf16[4,32,48,256]{3,2,1,0:T(8,128)(2,1)}), bf16[4,32,48,256]{3,2,1,0:T(8,128)(2,1)}, u32[]{:S(2)}, u32[]{:S(2)}) %all-to-all-start.1) | async-done | bytes 3145760 | tf_op jit(solution)/shard_map/all_to_all | solution.py:41
  219.8 3.7 all-to-all-start.10
  226.1 4.0 copy.92
  230.1 8.2 %all-to-all-done.10 = bf16[8,64,768]{2,1,0:T(8,128)(2,1)S(1)} async-done(((bf16[8,64,768]{2,1,0:T(8,128)(2,1)}), bf16[8,64,768]{2,1,0:T(8,128)(2,1)S(1)}, u32[]{:S(2)}, u32[]{:S(2)}) %all-to-all-start.10) | async-done | bytes 786464 | tf_op jit(solution)/shard_map/all_to_all | solution.py:41
  240.9 22.7 %all_to_all.160 = bf16[2,4,32,48,256]{4,3,1,2,0:T(8,128)(2,1)} all-to-all(bf16[2,4,32,48,256]{4,3,1,2,0:T(8,128)(2,1)S(1)} %broadcast_in_dim.37), channel_id=1, replica_groups=mesh['x'=4,'core'=2,'z'=8,'y'=4] {'core'}, dimensions={0} | all-to-all | bytes 12582912 | tf_op jit(solution)/shard_map/all_to_all | solution.py:41
  263.7 4.2 all-to-all-start.12
  268.3 5.1 %fusion.9 = (bf16[2,4,32,24,256]{4,3,1,2,0:T(8,128)(2,1)}, bf16[32,24,4,2,256]{4,1,2,0,3:T(8,128)(2,1)S(1)}) fusion(bf16[2,4,32,48,256]{4,3,1,2,0:T(8,128)(2,1)} %all_to_all.160), kind=kLoop, calls=%fused_computation.45 | loop fusion | bytes 12582912 | tf_op jit(solution)/shard_map/slice | solution.py:190
  273.4 4.9 %copy.93 = bf16[32,24,4,2,256]{4,3,2,1,0:T(2,128)(2,1)} copy(bf16[32,24,4,2,256]{4,1,2,0,3:T(8,128)(2,1)S(1)} %get-tuple-element.16) | data formatting | bytes 6291456 | tf_op jit(solution)/shard_map/transpose | solution.py:188
  278.3 6.1 %reshape.246 = bf16[768,2048]{1,0:T(8,128)(2,1)} reshape(bf16[32,24,4,2,256]{4,3,2,1,0:T(2,128)(2,1)} %copy.93) | data formatting | bytes 6291456 | tf_op jit(solution)/shard_map/reshape | solution.py:188
  294.5 6.8 %shard_map.86 = (f32[128,1]{1,0:T(8,128)S(1)}, bf16[128,768]{1,0:T(8,128)(2,1)S(1)}, bf16[2,4,512,384]{3,2,1,0:T(8,128)(2,1)}) custom-call(bf16[128,768]{1,0:T(8,128)(2,1)S(1)} %fusion.embedded_ref, bf16[128,768]{1,0:T(8,128)(2,1)S(1)} %copy-done.2, bf16[128,2048]{1,0:T(8,128)(2,1)S(1)} %get-tuple-element.26.hidden_ref, ...), custom_call_target="tpu_custom_call" | custom-call | tf_op jit(solution)/shard_map/pallas_call | solution.py:203
  302.0 10.4 %all_to_all.161 = bf16[2,4,512,384]{3,2,1,0:T(8,128)(2,1)} all-to-all(bf16[2,4,512,384]{3,2,1,0:T(8,128)(2,1)} %get-tuple-element.14), channel_id=1, replica_groups=mesh['x'=4,'core'=2,'z'=8,'y'=4] {'core'}, dimensions={0} | all-to-all | bytes 6291456 | tf_op jit(solution)/shard_map/all_to_all | solution.py:41
  312.3 4.2 reduce_sum.81
  316.5 4.6 %all-to-all-start.18 = ((bf16[4,512,384]{2,1,0:T(8,128)(2,1)}), bf16[4,512,384]{2,1,0:T(8,128)(2,1)}, u32[]{:S(2)}, u32[]{:S(2)}) async-start(bf16[4,512,384]{2,1,0:T(8,128)(2,1)} %reduce_sum.81), calls=%async_computation.18 | async-start | bytes 3145728 | tf_op jit(solution)/shard_map/all_to_all | solution.py:41
  321.1 6.0 %shard_map.87 = bf16[2,4,768,256]{3,2,1,0:T(8,128)(2,1)} custom-call(bf16[128,768]{1,0:T(8,128)(2,1)S(1)} %copy-done.1, bf16[128,768]{1,0:T(8,128)(2,1)S(1)} %copy-done.4, f32[128,2048]{1,0:T(8,128)S(1)} %copy-done, bf16[2048,768]{1,0:T(8,128)(2,1)} %bitcast.100), custom_call_target="tpu_custom_call" | custom-call | tf_op jit(solution)/shard_map/pallas_call | solution.py:211
  327.1 14.3 %all-to-all-done.18 = bf16[4,512,384]{2,1,0:T(8,128)(2,1)} async-done(((bf16[4,512,384]{2,1,0:T(8,128)(2,1)}), bf16[4,512,384]{2,1,0:T(8,128)(2,1)}, u32[]{:S(2)}, u32[]{:S(2)}) %all-to-all-start.18) | async-done | bytes 1572896 | tf_op jit(solution)/shard_map/all_to_all | solution.py:41
  341.4 6.4 %all-to-all-start.13 = ((bf16[2,4,768,256]{3,2,1,0:T(8,128)(2,1)}), bf16[2,4,768,256]{3,2,1,0:T(8,128)(2,1)}, u32[]{:S(2)}, u32[]{:S(2)}) async-start(bf16[2,4,768,256]{3,2,1,0:T(8,128)(2,1)} %shard_map.87), calls=%async_computation.13 | async-start | bytes 6291456 | tf_op jit(solution)/shard_map/all_to_all | solution.py:41
  354.7 4.0 reduce_sum.78
  358.7 3.8 all-to-all-done.19
  362.4 3.6 all-to-all-start.14
  366.7 18.8 %all-to-all-done.14 = bf16[4,768,256]{2,1,0:T(8,128)(2,1)S(1)} async-done(((bf16[4,768,256]{2,1,0:T(8,128)(2,1)}), bf16[4,768,256]{2,1,0:T(8,128)(2,1)S(1)}, u32[]{:S(2)}, u32[]{:S(2)}) %all-to-all-start.14) | async-done | bytes 1572896 | tf_op jit(solution)/shard_map/all_to_all | solution.py:41
  385.5 6.8 %all-to-all-start.20 = ((bf16[8,16,384]{2,1,0:T(8,128)(2,1)}), bf16[8,16,384]{2,1,0:T(8,128)(2,1)S(1)}, u32[]{:S(2)}, u32[]{:S(2)}) async-start(bf16[8,16,384]{2,1,0:T(8,128)(2,1)} %bitcast.48), calls=%async_computation.20 | async-start | bytes 196608 | tf_op jit(solution)/shard_map/all_to_all | solution.py:41
  393.4 6.5 %all-to-all-done.20 = bf16[8,16,384]{2,1,0:T(8,128)(2,1)S(1)} async-done(((bf16[8,16,384]{2,1,0:T(8,128)(2,1)}), bf16[8,16,384]{2,1,0:T(8,128)(2,1)S(1)}, u32[]{:S(2)}, u32[]{:S(2)}) %all-to-all-start.20) | async-done | bytes 98336 | tf_op jit(solution)/shard_map/all_to_all | solution.py:41
  399.9 3.9 all-to-all-start.15
  403.8 11.8 %all-to-all-done.15 = bf16[32,24,256]{2,1,0:T(8,128)(2,1)S(1)} async-done(((bf16[32,24,256]{2,1,0:T(8,128)(2,1)}), bf16[32,24,256]{2,1,0:T(8,128)(2,1)S(1)}, u32[]{:S(2)}, u32[]{:S(2)}) %all-to-all-start.15) | async-done | bytes 393248 | tf_op jit(solution)/shard_map/all_to_all | solution.py:41
  416.3 8.0 %all-to-all-start.21 = ((f32[8,16,384]{2,1,0:T(8,128)}), f32[8,16,384]{2,1,0:T(8,128)S(1)}, u32[]{:S(2)}, u32[]{:S(2)}) async-start(f32[8,16,384]{2,1,0:T(8,128)} %broadcast_in_dim.76), calls=%async_computation.21 | async-start | bytes 393216 | tf_op jit(solution)/shard_map/all_to_all | solution.py:41
  424.3 5.8 %all-to-all-done.21 = f32[8,16,384]{2,1,0:T(8,128)S(1)} async-done(((f32[8,16,384]{2,1,0:T(8,128)}), f32[8,16,384]{2,1,0:T(8,128)S(1)}, u32[]{:S(2)}, u32[]{:S(2)}) %all-to-all-start.21) | async-done | bytes 196640 | tf_op jit(solution)/shard_map/all_to_all | solution.py:41
  430.9 4.2 all-to-all-start.16
  436.5 4.5 %all-to-all-done.16 = f32[8,24,256]{2,1,0:T(8,128)S(1)} async-done(((f32[8,24,256]{2,1,0:T(8,128)}), f32[8,24,256]{2,1,0:T(8,128)S(1)}, u32[]{:S(2)}, u32[]{:S(2)}) %all-to-all-start.16) | async-done | bytes 196640 | tf_op jit(solution)/shard_map/all_to_all | solution.py:41
  (80 shorter events, 44.0 us)
Async XLA Ops:
  28.3 12.7 %all-to-all-start.3 = ((s32[8,2,128]{2,1,0:T(2,128)}), s32[8,2,128]{2,1,0:T(2,128)S(1)}, u32[]{:S(2)}, u32[]{:S(2)}) async-start(s32[8,2,128]{2,1,0:T(2,128)} %bitcast.7), calls=%async_computation.3 | async-start | bytes 16384 | tf_op jit(solution)/shard_map/all_to_all | solution.py:41
  41.1 22.2 %all-to-all-start.5 = ((bf16[4,256,768]{2,1,0:T(8,128)(2,1)}), bf16[4,256,768]{2,1,0:T(8,128)(2,1)S(1)}, u32[]{:S(2)}, u32[]{:S(2)}) async-start(bf16[4,256,768]{2,1,0:T(8,128)(2,1)} %bitcast.13), calls=%async_computation.5 | async-start | bytes 3145728 | tf_op jit(solution)/shard_map/all_to_all | solution.py:41
  63.2 21.3 %all-to-all-start.7 = ((bf16[4,256,768]{2,1,0:T(8,128)(2,1)}), bf16[4,256,768]{2,1,0:T(8,128)(2,1)S(1)}, u32[]{:S(2)}, u32[]{:S(2)}) async-start(bf16[4,256,768]{2,1,0:T(8,128)(2,1)} %bitcast.108), calls=%async_computation.7 | async-start | bytes 3145728 | tf_op jit(solution)/shard_map/all_to_all | solution.py:41
  84.5 1.2 copy-start.6
  85.7 20.0 %all-to-all-start.9 = ((bf16[4,256,768]{2,1,0:T(8,128)(2,1)}), bf16[4,256,768]{2,1,0:T(8,128)(2,1)S(1)}, u32[]{:S(2)}, u32[]{:S(2)}) async-start(bf16[4,256,768]{2,1,0:T(8,128)(2,1)} %bitcast.107), calls=%async_computation.9 | async-start | bytes 3145728 | tf_op jit(solution)/shard_map/all_to_all | solution.py:41
  98.5 11.6 %copy-start.8 = (bf16[64,768]{1,0:T(8,128)(2,1)S(1)}, bf16[64,768]{1,0:T(8,128)(2,1)}, u32[]{:S(2)}) copy-start(bf16[64,768]{1,0:T(8,128)(2,1)} %param.11) | copy-start | bytes 294916
  105.7 19.7 %all-to-all-start.11 = ((bf16[4,256,768]{2,1,0:T(8,128)(2,1)}), bf16[4,256,768]{2,1,0:T(8,128)(2,1)}, u32[]{:S(2)}, u32[]{:S(2)}) async-start(bf16[4,256,768]{2,1,0:T(8,128)(2,1)} %bitcast.106), calls=%async_computation.11 | async-start | bytes 3145728 | tf_op jit(solution)/shard_map/all_to_all | solution.py:41
  126.4 21.6 %all-to-all-start = ((bf16[32,48,256]{2,1,0:T(8,128)(2,1)}), bf16[32,48,256]{2,1,0:T(8,128)(2,1)}, u32[]{:S(2)}, u32[]{:S(2)}) async-start(bf16[32,48,256]{2,1,0:T(8,128)(2,1)} %broadcast_in_dim.35), calls=%async_computation | async-start | bytes 1572864 | tf_op jit(solution)/shard_map/all_to_all | solution.py:41
  148.0 19.1 %all-to-all-start.6 = ((bf16[8,64,768]{2,1,0:T(8,128)(2,1)}), bf16[8,64,768]{2,1,0:T(8,128)(2,1)S(1)}, u32[]{:S(2)}, u32[]{:S(2)}) async-start(bf16[8,64,768]{2,1,0:T(8,128)(2,1)} %bitcast.18), calls=%async_computation.6 | async-start | bytes 1572864 | tf_op jit(solution)/shard_map/all_to_all | solution.py:41
  188.6 31.3 %all-to-all-start.1 = ((bf16[4,32,48,256]{3,2,1,0:T(8,128)(2,1)}), bf16[4,32,48,256]{3,2,1,0:T(8,128)(2,1)}, u32[]{:S(2)}, u32[]{:S(2)}) async-start(bf16[4,32,48,256]{3,2,1,0:T(8,128)(2,1)} %broadcast_in_dim.36), calls=%async_computation.1 | async-start | bytes 6291456 | tf_op jit(solution)/shard_map/all_to_all | solution.py:41
  219.8 18.5 %all-to-all-start.10 = ((bf16[8,64,768]{2,1,0:T(8,128)(2,1)}), bf16[8,64,768]{2,1,0:T(8,128)(2,1)S(1)}, u32[]{:S(2)}, u32[]{:S(2)}) async-start(bf16[8,64,768]{2,1,0:T(8,128)(2,1)} %bitcast.35), calls=%async_computation.10 | async-start | bytes 1572864 | tf_op jit(solution)/shard_map/all_to_all | solution.py:41
  263.7 30.5 %all-to-all-start.12 = ((bf16[8,64,768]{2,1,0:T(8,128)(2,1)}), bf16[8,64,768]{2,1,0:T(8,128)(2,1)}, u32[]{:S(2)}, u32[]{:S(2)}) async-start(bf16[8,64,768]{2,1,0:T(8,128)(2,1)} %bitcast.43), calls=%async_computation.12 | async-start | bytes 1572864 | tf_op jit(solution)/shard_map/all_to_all | solution.py:41
  289.6 0.9 copy-start.1
  289.6 2.0 copy-start.7
  291.6 2.0 copy-start.5
  293.5 0.9 copy-start.2
  301.3 0.7 copy-start.3
  312.3 8.7 %copy-start = (f32[128,2048]{1,0:T(8,128)S(1)}, f32[128,2048]{1,0:T(8,128)}, u32[]{:S(2)}) copy-start(f32[128,2048]{1,0:T(8,128)} %get-tuple-element.25.slope_ref) | copy-start | bytes 3145732
  312.3 8.8 %copy-start.4 = (bf16[128,768]{1,0:T(8,128)(2,1)S(1)}, bf16[128,768]{1,0:T(8,128)(2,1)}, u32[]{:S(2)}) copy-start(bf16[128,768]{1,0:T(8,128)(2,1)} %copy-done.3) | copy-start | bytes 589828
  316.5 24.9 %all-to-all-start.18 = ((bf16[4,512,384]{2,1,0:T(8,128)(2,1)}), bf16[4,512,384]{2,1,0:T(8,128)(2,1)}, u32[]{:S(2)}, u32[]{:S(2)}) async-start(bf16[4,512,384]{2,1,0:T(8,128)(2,1)} %reduce_sum.81), calls=%async_computation.18 | async-start | bytes 3145728 | tf_op jit(solution)/shard_map/all_to_all | solution.py:41
  341.4 9.8 %all-to-all-start.13 = ((bf16[2,4,768,256]{3,2,1,0:T(8,128)(2,1)}), bf16[2,4,768,256]{3,2,1,0:T(8,128)(2,1)}, u32[]{:S(2)}, u32[]{:S(2)}) async-start(bf16[2,4,768,256]{3,2,1,0:T(8,128)(2,1)} %shard_map.87), calls=%async_computation.13 | async-start | bytes 6291456 | tf_op jit(solution)/shard_map/all_to_all | solution.py:41
  351.2 11.3 %all-to-all-start.19 = ((bf16[4,128,384]{2,1,0:T(8,128)(2,1)}), bf16[4,128,384]{2,1,0:T(8,128)(2,1)S(1)}, u32[]{:S(2)}, u32[]{:S(2)}) async-start(bf16[4,128,384]{2,1,0:T(8,128)(2,1)} %bitcast.47), calls=%async_computation.19 | async-start | bytes 786432 | tf_op jit(solution)/shard_map/all_to_all | solution.py:41
  362.4 23.1 %all-to-all-start.14 = ((bf16[4,768,256]{2,1,0:T(8,128)(2,1)}), bf16[4,768,256]{2,1,0:T(8,128)(2,1)S(1)}, u32[]{:S(2)}, u32[]{:S(2)}) async-start(bf16[4,768,256]{2,1,0:T(8,128)(2,1)} %reduce_sum.78), calls=%async_computation.14 | async-start | bytes 3145728 | tf_op jit(solution)/shard_map/all_to_all | solution.py:41
  385.5 14.4 %all-to-all-start.20 = ((bf16[8,16,384]{2,1,0:T(8,128)(2,1)}), bf16[8,16,384]{2,1,0:T(8,128)(2,1)S(1)}, u32[]{:S(2)}, u32[]{:S(2)}) async-start(bf16[8,16,384]{2,1,0:T(8,128)(2,1)} %bitcast.48), calls=%async_computation.20 | async-start | bytes 196608 | tf_op jit(solution)/shard_map/all_to_all | solution.py:41
  399.9 15.7 %all-to-all-start.15 = ((bf16[32,24,256]{2,1,0:T(8,128)(2,1)}), bf16[32,24,256]{2,1,0:T(8,128)(2,1)S(1)}, u32[]{:S(2)}, u32[]{:S(2)}) async-start(bf16[32,24,256]{2,1,0:T(8,128)(2,1)} %bitcast.45), calls=%async_computation.15 | async-start | bytes 786432 | tf_op jit(solution)/shard_map/all_to_all | solution.py:41
  416.3 13.9 %all-to-all-start.21 = ((f32[8,16,384]{2,1,0:T(8,128)}), f32[8,16,384]{2,1,0:T(8,128)S(1)}, u32[]{:S(2)}, u32[]{:S(2)}) async-start(f32[8,16,384]{2,1,0:T(8,128)} %broadcast_in_dim.76), calls=%async_computation.21 | async-start | bytes 393216 | tf_op jit(solution)/shard_map/all_to_all | solution.py:41
  430.9 10.2 %all-to-all-start.16 = ((f32[8,24,256]{2,1,0:T(8,128)}), f32[8,24,256]{2,1,0:T(8,128)S(1)}, u32[]{:S(2)}, u32[]{:S(2)}) async-start(f32[8,24,256]{2,1,0:T(8,128)} %broadcast_in_dim.75), calls=%async_computation.16 | async-start | bytes 393216 | tf_op jit(solution)/shard_map/all_to_all | solution.py:41
